TPU v7x, 32 devices: a whole 2x2x4 slice. The times are simulated.
32 devices in a mesh: ctx: 16 (over z, x, core), exp: 2 (over y).
Axes of the slice: x: 2, y: 2, z: 4, core: 2. Of those that a mesh axis runs over, the one named last changes fastest.
Arguments:
- queries: bfloat16 [1024, 6144], P('ctx', 'exp'), may hold values from -23 to 23
- projected_key_value: bfloat16 [1024, 2, 1024], P('ctx', None, 'exp'), may hold values from -6 to 6
- doc_ids: int32 [1024], P('ctx'), may hold values from 0 to 7, never falling along the last dimension, each value on 1 to 768 neighbouring positions
- residual_in: bfloat16 [1024, 6144], P('exp', 'ctx'), may hold values from -6 to 6
- out_proj: bfloat16 [6144, 6144], P('exp', 'ctx'), may hold values from -0.3125 to 0.3125
- norm_gain: bfloat16 [6144], P('ctx'), may hold values from 0.25 to 1.75
- expert_ids: int32 [1024, 2], replicated, may hold values from 0 to 7, all different within a row; in each aligned block of 512 rows (0 to 511, 512 to 1023, ...) at most 144 rows name the same one
- route_weights: float32 [1024, 2], replicated, may hold values from 0.2 to 1
- gate_proj: bfloat16 [8, 6144, 8192], P('exp', None, 'ctx'), may hold values from -0.078125 to 0.078125
- up_proj: bfloat16 [8, 6144, 8192], P('exp', None, 'ctx'), may hold values from -0.078125 to 0.078125
- down_proj: bfloat16 [8, 8192, 6144], P('exp', None, 'ctx'), may hold values from -0.0625 to 0.0625
Outputs:
- mixed: bfloat16 [1024, 6144], P('exp', 'ctx')
Inputs may be any that keep to these rules, and one draw needn't show every extreme that they name: `expert_ids`: in each aligned block of 512 rows no expert is named by more than 144 rows, a bound that some block reaches; each row names 2 different experts. `doc_ids`: document numbers never fall along the window; a document has at most 768 positions and one has exactly that many.
All inputs are finite; a program needn't handle non-finite values.
Results may differ from a plain program's by a relative error of at most 0.018.
Values may be sent and summed in bfloat16 or wider, within the bound.
A program may use at most 192 MiB of HBM per device.

v0:
```python
import math

import jax
import jax.numpy as jnp
from jax import lax
from jax.sharding import PartitionSpec as P

QUERY_HEADS = 48
KEY_VALUE_HEADS = 8
HEAD_WIDTH = 128
EXPERTS = 8


NEG = -1e30


def routing_tables(expert_ids, route_weights, n_experts, n_blocks):
    seq_len = expert_ids.shape[0]
    rows_block = seq_len // n_blocks
    capacity = rows_block * 9 // 32
    labels = jnp.arange(n_experts, dtype=jnp.int32)
    onehot = (expert_ids[:, :, None] == labels[None, None, :]).astype(jnp.int32)
    hits = jnp.sum(onehot, axis=1).reshape(n_blocks, rows_block, n_experts)
    before = (jnp.cumsum(hits, axis=1) - hits).reshape(seq_len, n_experts)
    rank = jnp.sum(onehot * before[:, None, :], axis=2)
    position = jnp.arange(seq_len, dtype=jnp.int32)
    slot = (position // rows_block)[:, None] * capacity + rank
    width = n_blocks * capacity
    owners = jnp.broadcast_to(position[:, None], expert_ids.shape)
    tok_of = jnp.zeros((n_experts, width), jnp.int32).at[expert_ids, slot].set(owners)
    valid = jnp.zeros((n_experts, width), jnp.float32).at[expert_ids, slot].set(1.0)
    weight = jnp.zeros((n_experts, width), jnp.float32).at[expert_ids, slot].set(route_weights)
    first = jnp.zeros((n_experts, width), jnp.float32).at[expert_ids[:, 0], slot[:, 0]].set(1.0)
    return (tok_of, valid, weight, first)


def on_device(
    queries,
    projected_key_value,
    doc_ids,
    residual_in,
    out_proj,
    norm_gain,
    expert_ids,
    route_weights,
    gate_proj,
    up_proj,
    down_proj,
):
    tok_count = queries.shape[0]
    head_groups = QUERY_HEADS // KEY_VALUE_HEADS
    kv_local = projected_key_value.shape[2] // HEAD_WIDTH
    scale = 1.0 / math.sqrt(HEAD_WIDTH)
    heads_of_queries = queries.reshape(tok_count, kv_local, head_groups, HEAD_WIDTH)
    query_pos = lax.axis_index("ctx") * tok_count + jnp.arange(tok_count, dtype=jnp.int32)
    kv_piece = lax.all_gather(projected_key_value, "ctx", axis=0, tiled=True)
    doc_piece = lax.all_gather(doc_ids, "ctx", axis=0, tiled=True)
    key_rows = kv_piece.shape[0]
    heads_of_keys = kv_piece[:, 0].reshape(key_rows, kv_local, HEAD_WIDTH)
    heads_of_values = kv_piece[:, 1].reshape(key_rows, kv_local, HEAD_WIDTH)
    key_pos = jnp.arange(key_rows, dtype=jnp.int32)
    visible = (doc_ids[:, None] == doc_piece[None, :]) & (key_pos[None, :] <= query_pos[:, None])
    running = jnp.full((kv_local, head_groups, tok_count), NEG, jnp.float32)
    scores = (
        jnp.einsum(
            "tkgd,skd->kgts", heads_of_queries, heads_of_keys, preferred_element_type=jnp.float32
        )
        * scale
    )
    scores = jnp.where(visible, scores, NEG)
    newmax = jnp.maximum(running, jnp.max(scores, axis=-1))
    expo = jnp.where(visible, jnp.exp(scores - newmax[..., None]), 0.0)
    total_new = jnp.sum(expo, axis=-1)
    weights = expo.astype(jnp.bfloat16)
    product = jnp.einsum(
        "kgts,skd->kgtd", weights, heads_of_values, preferred_element_type=jnp.float32
    )
    attended = (
        (product / total_new[..., None])
        .transpose(2, 0, 1, 3)
        .reshape(tok_count, -1)
        .astype(jnp.bfloat16)
    )
    partial_out = jnp.dot(
        lax.all_gather(attended, "ctx", axis=0, tiled=True),
        out_proj,
        preferred_element_type=jnp.float32,
    )
    n_blocks = lax.axis_size("exp")
    block_index = lax.axis_index("exp")
    seq_len = expert_ids.shape[0]
    rows_block = seq_len // n_blocks
    capacity = rows_block * 9 // 32
    feat_local = partial_out.shape[1]
    local_experts = gate_proj.shape[0]
    tok_of, valid, weight, first = routing_tables(expert_ids, route_weights, EXPERTS, n_blocks)
    my_valid = lax.dynamic_slice_in_dim(valid, block_index * local_experts, local_experts, 0)
    my_weight = lax.dynamic_slice_in_dim(weight, block_index * local_experts, local_experts, 0)
    my_first = lax.dynamic_slice_in_dim(first, block_index * local_experts, local_experts, 0)
    block_tok = (
        lax.dynamic_index_in_dim(
            tok_of.reshape(EXPERTS, n_blocks, capacity), block_index, 1, keepdims=False
        )
        - block_index * rows_block
    )
    block_valid = lax.dynamic_index_in_dim(
        valid.reshape(EXPERTS, n_blocks, capacity), block_index, 1, keepdims=False
    )
    own_rows = lax.dynamic_slice_in_dim(
        partial_out, block_index * rows_block, rows_block, 0
    ) + residual_in.astype(jnp.float32)
    with_base = lax.dynamic_update_slice_in_dim(partial_out, own_rows, block_index * rows_block, 0)
    shares = jnp.take(with_base, tok_of, axis=0) * valid[..., None]
    received = lax.all_to_all(
        shares.astype(jnp.bfloat16), "exp", split_axis=0, concat_axis=1, tiled=True
    ).astype(shares.dtype)
    summed = jnp.sum(received.reshape(local_experts, n_blocks, -1, feat_local), axis=1)
    expert_rows = jnp.where(my_valid[..., None] > 0, summed, 0.0).astype(jnp.bfloat16)
    full_rows, full_gain = (
        lax.all_gather(expert_rows, "ctx", axis=2, tiled=True),
        lax.all_gather(norm_gain, "ctx", axis=0, tiled=True),
    )
    meansq = (
        jnp.einsum("erd,erd->er", full_rows, full_rows, preferred_element_type=jnp.float32)
        / full_rows.shape[2]
    )
    inverse = lax.rsqrt(meansq + 1e-05)
    normed = (
        full_rows.astype(jnp.float32) * inverse[..., None] * full_gain.astype(jnp.float32)
    ).astype(jnp.bfloat16)
    gate = jnp.einsum("erd,edf->erf", normed, gate_proj, preferred_element_type=jnp.float32)
    upper = jnp.einsum("erd,edf->erf", normed, up_proj, preferred_element_type=jnp.float32)
    hidden = (jax.nn.silu(gate) * upper).astype(jnp.bfloat16)
    expert_out = jnp.einsum(
        "erf,efd->erd",
        lax.all_gather(hidden, "ctx", axis=2, tiled=True),
        down_proj,
        preferred_element_type=jnp.float32,
    )
    payload = my_weight[..., None] * expert_out + my_first[..., None] * expert_rows.astype(
        jnp.float32
    )
    back = lax.all_to_all(
        payload.reshape(local_experts, n_blocks, capacity, feat_local).astype(jnp.bfloat16),
        "exp",
        split_axis=1,
        concat_axis=0,
        tiled=True,
    ).astype(jnp.float32)
    back = back.reshape(EXPERTS * capacity, feat_local)
    row_labels = jnp.arange(rows_block, dtype=jnp.int32)
    picker = (
        (block_tok.reshape(-1)[None, :] == row_labels[:, None])
        & (block_valid.reshape(-1)[None, :] > 0)
    ).astype(jnp.float32)
    mixed = jnp.dot(picker, back, precision=lax.Precision.HIGHEST)
    return mixed.astype(jnp.bfloat16)


def solution(mesh):
    placed = (
        P("ctx", "exp"),
        P("ctx", None, "exp"),
        P("ctx"),
        P("exp", "ctx"),
        P("exp", "ctx"),
        P("ctx"),
        P(),
        P(),
        P("exp", None, "ctx"),
        P("exp", None, "ctx"),
        P("exp", None, "ctx"),
    )
    return jax.shard_map(
        on_device, mesh=mesh, in_specs=placed, out_specs=P("exp", "ctx"), check_vma=False
    )
```

profile of v0, /device:TPU:0, one launch (start us, length us, event | category | flops | bytes accessed | tf_op | source)
XLA Modules:
  0.0 488.8 jit_solution(3748327597280672574)
XLA Ops:
  6.5 0.7 all-gather.6.cloned.1.call-update
  7.3 2.3 reshape.131
  9.6 1.2 dynamic-slice
  11.5 0.9 dynamic-update-slice
  12.4 13.7 %all-reduce = s32[1024]{0:T(1024)S(1)} all-reduce(s32[1024]{0:T(1024)S(1)} %dynamic-update-slice), channel_id=1, replica_groups=mesh['ctx'=16,'exp'=2] {'ctx'}, use_global_device_ids=true, to_apply=%add | all-reduce | flops 1024 | bytes 8192
  26.1 0.8 fusion.34
  26.9 26.8 %all-gather.6.cloned.1.call-done = bf16[1024,2,512]{2,1,0:T(2,128)(2,1)} async-done(((bf16[64,2,512]{2,1,0:T(2,128)(2,1)}), bf16[1024,2,512]{2,1,0:T(2,128)(2,1)}) %all-gather.6.cloned.1.call-update) | async-done | bytes 2097168 | tf_op jit(solution)/shard_map/all_gather | solution.py:56
  53.7 6.8 %fusion.51 = (bf16[1024,1,512]{2,1,0:T(2,128)(2,1)}, bf16[1024,1,512]{2,1,0:T(2,128)(2,1)}) fusion(bf16[1024,2,512]{2,1,0:T(2,128)(2,1)} %all-gather.6.cloned.1.call-done), kind=kLoop, calls=%fused_computation.88 | loop fusion | bytes 4194304 | tf_op jit(solution)/shard_map/slice | solution.py:59
  60.5 4.6 copy.61
  65.0 5.8 %copy.62 = bf16[1024,1,512]{0,2,1:T(8,128)(2,1)} copy(bf16[1024,1,512]{2,1,0:T(2,128)(2,1)} %get-tuple-element.6) | data formatting | bytes 2097152
  70.9 2.5 fusion.7
  73.4 2.0 fusion.8
  75.4 1.8 fusion.29
  77.2 0.3 copy.49
  77.5 1.2 convert_element_type.58
  78.7 2.3 reduce-window.6
  81.0 0.3 slice_reduce_fusion
  81.7 0.4 copy-done.9
  82.3 0.3 reshape.160
  82.6 8.1 %scatter_custom_fusion.1 = f32[2304]{0:T(1024)S(1)} fusion(s32[2048]{0:T(1024)S(1)} %reshape.160, f32[2048]{0:T(1024)S(1)} %broadcast.176, f32[]{:T(128)} %constant.46.clone.1), kind=kCustom, calls=%fused_computation.68 | custom fusion | bytes 9220
  90.6 0.7 reshape.140
  91.3 0.3 reshape.162
  91.6 8.2 %scatter_custom_fusion = s32[2304]{0:T(1024)S(1)} fusion(s32[2048]{0:T(1024)S(1)} %reshape.160, s32[2048]{0:T(1024)S(1)} %reshape.162, s32[]{:T(128)} %constant.28.clone.1), kind=kCustom, calls=%fused_computation.70 | custom fusion | bytes 9220
  100.0 0.6 pad_clamp_fusion
  100.6 0.6 compare_and_fusion
  101.2 38.2 %all-gather.8.cloned.1.call-done = bf16[1024,3072]{1,0:T(8,128)(2,1)} async-done(((bf16[64,3072]{1,0:T(8,128)(2,1)}), bf16[1024,3072]{1,0:T(8,128)(2,1)}) %all-gather.8.cloned.1.call-update) | async-done | bytes 6291472 | tf_op jit(solution)/shard_map/all_gather | solution.py:85
  139.5 6.6 %fusion.52 = f32[1024,384]{1,0:T(8,128)} fusion(bf16[1024,3072]{1,0:T(8,128)(2,1)} %all-gather.8.cloned.1.call-done, bf16[3072,384]{1,0:T(8,128)(2,1)S(1)} %copy-done), kind=kOutput, calls=%fused_computation.89 | convolution fusion | flops 2415919104 | bytes 10223616 | tf_op jit(solution)/shard_map/dot_general | solution.py:84
  146.1 2.1 add_dynamic-update-slice_fusion
  148.2 8.0 %gather_fusion = f32[2304,384]{1,0:T(8,128)S(1)} fusion(f32[1024,384]{1,0:T(8,128)} %add_dynamic-update-slice_fusion, s32[3072]{0:T(1024)} %pad_clamp_fusion), kind=kCustom, calls=%fused_computation | custom fusion | bytes 7087104 | tf_op jit(solution)/shard_map/jit(_take)/gather | solution.py:113
  156.2 2.4 multiply_convert_fusion
  158.6 3.8 all-to-all-start
  162.5 0.7 dynamic-slice_compare_fusion
  163.2 21.2 %all-to-all-done = bf16[8,288,384]{2,1,0:T(8,128)(2,1)S(1)} async-done(((bf16[8,288,384]{2,1,0:T(8,128)(2,1)}), bf16[8,288,384]{2,1,0:T(8,128)(2,1)S(1)}, u32[]{:S(2)}, u32[]{:S(2)}) %all-to-all-start) | async-done | bytes 1769504 | tf_op jit(solution)/shard_map/all_to_all | solution.py:114
  184.7 1.3 select_convert_fusion
  186.1 19.5 %all-gather = bf16[16,1,384]{2,1,0:T(2,128)(2,1)S(1)} all-gather(bf16[1,1,384]{2,1,0:T(2,128)(2,1)S(1)} %reshape.189), channel_id=1, replica_groups=mesh['ctx'=16,'exp'=2] {'ctx'}, dimensions={0}, use_global_device_ids=true | all-gather | bytes 13056 | tf_op jit(solution)/shard_map/all_gather | solution.py:121
  205.6 92.2 %all-gather.10.cloned.1.call-done = bf16[4,288,6144]{2,1,0:T(8,128)(2,1)} async-done(((bf16[4,288,384]{2,1,0:T(8,128)(2,1)}), bf16[4,288,6144]{2,1,0:T(8,128)(2,1)}) %all-gather.10.cloned.1.call-update) | async-done | bytes 14155792 | tf_op jit(solution)/shard_map/all_gather | solution.py:120
  297.8 7.8 %fusion.2 = f32[4,288]{1,0:T(4,128)S(1)} fusion(bf16[4,288,6144]{2,1,0:T(8,128)(2,1)} %all-gather.10.cloned.1.call-done), kind=kLoop, calls=%fused_computation.9 | loop fusion | flops 21232512 | bytes 14160384 | tf_op jit(solution)/shard_map/erd,erd->er/dot_general | solution.py:124
  305.6 18.0 %fusion.3 = f32[4,288,512]{2,1,0:T(8,128)S(1)} fusion(bf16[4,6144,512]{2,1,0:T(8,128)(2,1)} %param.20, bf16[4,288,6144]{2,1,0:T(8,128)(2,1)} %all-gather.10.cloned.1.call-done, f32[6144]{0:T(1024)S(1)} %bitcast.83, f32[4,288]{1,0:T(4,128)S(1)} %add_rsqrt_fusion), kind=kOutput, calls=%fused_computation.10 | convolution fusion | flops 7276068864 | bytes 41710080 | tf_op jit(solution)/shard_map/erd,edf->erf/dot_general | solution.py:132
  323.7 19.4 %multiply_convert_fusion.1 = bf16[4,288,512]{2,1,0:T(8,128)(2,1)} fusion(f32[4,288,512]{2,1,0:T(8,128)S(1)} %fusion.3, bf16[4,6144,512]{2,1,0:T(8,128)(2,1)} %param.19, bf16[4,288,6144]{2,1,0:T(8,128)(2,1)} %all-gather.10.cloned.1.call-done, f32[6144]{0:T(1024)S(1)} %bitcast.84, f32[4,288]{1,0:T(4,128)S(1)} %add_rsqrt_fusion), kind=kOutput, calls=%fused_computation.21 | convolution fusion | flops 7279607808 | bytes 42889728 | tf_op jit(solution)/shard_map/erd,edf->erf/dot_general | solution.py:131
  343.4 4.5 scatter_custom_fusion.3
  348.3 0.3 reshape.174
  348.5 8.2 %scatter_custom_fusion.2 = f32[2304]{0:T(1024)S(1)} fusion(s32[2048]{0:T(1024)} %copy-done.12, f32[2048]{0:T(1024)S(1)} %reshape.174, f32[]{:T(128)} %constant.46.clone.1), kind=kCustom, calls=%fused_computation.66 | custom fusion | bytes 9728
  356.8 83.6 %all-gather.12.cloned.1.call-done = bf16[4,288,8192]{2,1,0:T(8,128)(2,1)} async-done(((bf16[4,288,512]{2,1,0:T(8,128)(2,1)}), bf16[4,288,8192]{2,1,0:T(8,128)(2,1)}) %all-gather.12.cloned.1.call-update) | async-done | bytes 18874384 | tf_op jit(solution)/shard_map/all_gather | solution.py:136
  440.4 22.1 %add_convert_fusion = bf16[4,288,384]{2,1,0:T(8,128)(2,1)} fusion(bf16[4,288,384]{2,1,0:T(8,128)(2,1)S(1)} %copy-done.2, bf16[4,288,8192]{2,1,0:T(8,128)(2,1)} %all-gather.12.cloned.1.call-done, bf16[4,8192,384]{2,1,0:T(8,128)(2,1)} %param.21, f32[4,288]{1,0:T(4,128)S(1)} %get-tuple-element.9, f32[4,288]{1,0:T(4,128)S(1)} %get-tuple-element.10), kind=kOutput, calls=%fused_computation.25 | convolution fusion | flops 7249969152 | bytes 45818880 | tf_op jit(solution)/shard_map/erf,efd->erd/dot_general | solution.py:134
  462.5 2.2 copy.50
  464.6 3.6 all-to-all-start.1
  468.7 12.1 %all-to-all-done.1 = bf16[4,2,144,384]{3,2,0,1:T(8,128)(2,1)S(1)} async-done(((bf16[4,2,144,384]{3,2,0,1:T(8,128)(2,1)}), bf16[4,2,144,384]{3,2,0,1:T(8,128)(2,1)S(1)}, u32[]{:S(2)}, u32[]{:S(2)}) %all-to-all-start.1) | async-done | bytes 884768 | tf_op jit(solution)/shard_map/all_to_all | solution.py:143
  480.7 1.5 fusion.21
  (82 shorter events, 2.3 us)
Async XLA Ops:
  6.5 132.9 %copy-start = (bf16[3072,384]{1,0:T(8,128)(2,1)S(1)}, bf16[3072,384]{1,0:T(8,128)(2,1)}, u32[]{:S(2)}) copy-start(bf16[3072,384]{1,0:T(8,128)(2,1)} %param.15) | copy-start | bytes 7077892
  6.5 47.1 %all-gather.6.cloned.1.call-start = ((), (), s32[]{:S(2)}) async-start(), calls=%async_computation.2 | async-start | bytes 2228224 | tf_op jit(solution)/shard_map/all_gather | solution.py:56
  7.3 132.2 %all-gather.8.cloned.1.call-start = ((), (), s32[]{:S(2)}) async-start(), calls=%async_computation.3 | async-start | bytes 6684672 | tf_op jit(solution)/shard_map/all_gather | solution.py:85
  70.9 4.5 copy-start.3
  75.4 3.3 copy-start.7
  75.4 6.1 %copy-start.13 = (s32[2]{0:T(128)S(1)}, s32[2]{0:T(128)}, u32[]{:S(2)}) copy-start(s32[2]{0:T(128)} %constant.95) | copy-start | bytes 28
  75.4 6.2 %copy-start.15 = (s32[2]{0:T(128)S(1)}, s32[2]{0:T(128)}, u32[]{:S(2)}) copy-start(s32[2]{0:T(128)} %constant.98) | copy-start | bytes 28
  81.4 0.6 copy-start.9
  82.6 63.5 %copy-start.12 = (s32[2048]{0:T(1024)}, s32[2048]{0:T(1024)S(1)}, u32[]{:S(2)}) copy-start(s32[2048]{0:T(1024)S(1)} %reshape.160) | copy-start | bytes 24580
  99.9 0.8 copy-start.5
  101.2 44.9 %copy-start.4 = (bf16[512,384]{1,0:T(8,128)(2,1)S(1)}, bf16[512,384]{1,0:T(8,128)(2,1)}, u32[]{:S(2)}) copy-start(bf16[512,384]{1,0:T(8,128)(2,1)} %param.14) | copy-start | bytes 1179652
  158.6 27.5 %copy-start.17 = (bf16[384]{0:T(512)(128)(2,1)S(1)}, bf16[384]{0:T(512)(128)(2,1)}, u32[]{:S(2)}) copy-start(bf16[384]{0:T(512)(128)(2,1)} %param.16) | copy-start | bytes 2308
  158.6 25.8 %all-to-all-start = ((bf16[8,288,384]{2,1,0:T(8,128)(2,1)}), bf16[8,288,384]{2,1,0:T(8,128)(2,1)S(1)}, u32[]{:S(2)}, u32[]{:S(2)}) async-start(bf16[8,288,384]{2,1,0:T(8,128)(2,1)} %multiply_convert_fusion), calls=%async_computation | async-start | bytes 3538944 | tf_op jit(solution)/shard_map/all_to_all | solution.py:114
  162.4 135.4 %all-gather.10.cloned.1.call-start = ((), (), s32[]{:S(2)}) async-start(), calls=%async_computation.4 | async-start | bytes 15040512 | tf_op jit(solution)/shard_map/all_gather | solution.py:120
  186.0 254.4 %all-gather.12.cloned.1.call-start = ((), (), s32[]{:S(2)}) async-start(), calls=%async_computation.5 | async-start | bytes 20054016 | tf_op jit(solution)/shard_map/all_gather | solution.py:136
  323.7 19.5 %copy-start.8 = (s32[1024,2]{0,1:T(2,128)S(1)}, s32[1024,2]{0,1:T(2,128)}, u32[]{:S(2)}) copy-start(s32[1024,2]{0,1:T(2,128)} %param.17) | copy-start | bytes 24580
  323.7 19.5 %copy-start.10 = (s32[1024,2]{0,1:T(2,128)S(1)}, s32[1024,2]{0,1:T(2,128)}, u32[]{:S(2)}) copy-start(s32[1024,2]{0,1:T(2,128)} %copy-done.9) | copy-start | bytes 24580
  323.7 19.5 %copy-start.14 = (s32[2]{0:T(128)S(1)}, s32[2]{0:T(128)}, u32[]{:S(2)}) copy-start(s32[2]{0:T(128)} %constant.95) | copy-start | bytes 28
  323.7 19.6 %copy-start.16 = (s32[2]{0:T(128)S(1)}, s32[2]{0:T(128)}, u32[]{:S(2)}) copy-start(s32[2]{0:T(128)} %constant.98) | copy-start | bytes 28
  323.7 24.3 %copy-start.11 = (f32[1024,2]{0,1:T(2,128)S(1)}, f32[1024,2]{0,1:T(2,128)}, u32[]{:S(2)}) copy-start(f32[1024,2]{0,1:T(2,128)} %param.18) | copy-start | bytes 24580
  323.7 116.7 %copy-start.2 = (bf16[4,288,384]{2,1,0:T(8,128)(2,1)S(1)}, bf16[4,288,384]{2,1,0:T(8,128)(2,1)}, u32[]{:S(2)}) copy-start(bf16[4,288,384]{2,1,0:T(8,128)(2,1)} %select_convert_fusion) | copy-start | bytes 2654212
  440.4 27.9 %copy-start.6 = (s32[2304]{0:T(1024)S(1)}, s32[2304]{0:T(1024)}, u32[]{:S(2)}) copy-start(s32[2304]{0:T(1024)} %copy-done.5) | copy-start | bytes 27652
  440.4 41.9 %copy-start.1 = (bf16[3072,384]{1,0:T(8,128)(2,1)S(1)}, bf16[3072,384]{1,0:T(8,128)(2,1)}, u32[]{:S(2)}) copy-start(bf16[3072,384]{1,0:T(8,128)(2,1)} %param.15) | copy-start | bytes 7077892
  464.6 16.1 %all-to-all-start.1 = ((bf16[4,2,144,384]{3,2,0,1:T(8,128)(2,1)}), bf16[4,2,144,384]{3,2,0,1:T(8,128)(2,1)S(1)}, u32[]{:S(2)}, u32[]{:S(2)}) async-start(bf16[4,2,144,384]{3,2,0,1:T(8,128)(2,1)} %copy.50), calls=%async_computation.1 | async-start | bytes 1769472 | tf_op jit(solution)/shard_map/all_to_all | solution.py:143
Sparse Core Ops, SparseCore 0:
  9.5 44.1 all-gather.5
  78.8 60.6 all-gather.7
  186.1 111.6 all-gather.9
  343.2 97.1 all-gather.11
where the time goes:
time: 490 us; the launch traced here: 489 us
  waiting for transfers between devices  275 us (56%)
  matrix products  71.8 us (15%)
  local copies, waits for them, and re-layouts  65.6 us (13%)
  blocking collectives  33.2 us (7%)
  other arithmetic  21.6 us (4%)
  between operations  14.2 us (3%)
  starting transfers between devices  7.51 us (2%)
    all_gather x1, waiting for transfers between devices, on_device(): lax.all_gather(expert_rows, 'ctx', axis=2, tiled=True)  92.2 us
    all_gather x1, waiting for transfers between devices, on_device(): lax.all_gather(hidden, 'ctx', axis=2, tiled=True)  83.6 us
    unnamed x51, local copies, waits for them, and re-layouts  43 us
    all_gather x1, waiting for transfers between devices, on_device(): lax.all_gather(attended, 'ctx', axis=0, tiled=True)  38.2 us
    all_gather x1, waiting for transfers between devices, on_device(): kv_piece = lax.all_gather(projected_key_value, 'ctx', axis=0, tiled=True)  26.8 us
    dot_general x1, matrix products, on_device(): jnp.einsum('erf,efd->erd', lax.all_gather(hidden, 'ctx', axis=2, tiled=Tr...  22.1 us
    all_to_all x1, waiting for transfers between devices, on_device(): lax.all_to_all(shares.astype(jnp.bfloat16), 'exp', split_axis=0, concat_a...  21.2 us
    all_gather x1, blocking collectives, on_device(): lax.all_gather(norm_gain, 'ctx', axis=0, tiled=True)  19.5 us
  transfers between devices with their start and end apart: 6, of which 6 were waited for; matrix products, arithmetic and copies ran while one was open for 9% of the time, Pallas kernels for 0%

commit v1 on v0

v1 whole, which is shorter than its diff:
```python
import functools
import math

import jax
import jax.numpy as jnp
from jax import lax
from jax.experimental import pallas as pl
from jax.experimental.pallas import tpu as pltpu
from jax.sharding import PartitionSpec as P

QUERY_HEADS = 48
KEY_VALUE_HEADS = 8
HEAD_WIDTH = 128
EXPERTS = 8
NEG = -1e30

CHIPS = 8
RING_SIZE = 2 * CHIPS
MIB = 1 << 20


def chip_of(pos):
    x = pos // 4
    z = pos * (1 - x) + (CHIPS - 1 - pos) * x
    return z * 2 + x


def ring_place():
    me = lax.axis_index("ctx")
    core = lax.rem(me, 2)
    x = lax.rem(me // 2, 2)
    z = me // 4
    return z * (1 - x) + (CHIPS - 1 - z) * x, core


def ring_gather(x_ref, buf, sems, consume=None, ahead=None):
    local_sem, send_r, recv_r, send_l, recv_l, send_s, recv_s = sems
    pos, core = ring_place()

    def at(offset, c):
        return chip_of(lax.rem(pos + offset + CHIPS, CHIPS)) * 2 + c

    me = at(0, core)
    right, left, sibling = at(1, core), at(-1, core), at(0, 1 - core)
    half = x_ref.shape[0] // 2

    own = pltpu.make_async_copy(x_ref, buf.at[me], local_sem)
    own.start()
    barrier = pltpu.get_barrier_semaphore()
    for other in (right, left, sibling):
        pl.semaphore_signal(
            barrier, inc=1, device_id={"ctx": other}, device_id_type=pl.DeviceIdType.MESH
        )
    if ahead is not None:
        ahead(me)
    pl.semaphore_wait(barrier, 3)
    own.wait()

    def copy(origin, target, send, recv, part=None):
        view = buf.at[origin]
        if part is not None:
            view = buf.at[origin, pl.ds(part * half, half)]
        return pltpu.make_async_remote_copy(
            src_ref=view,
            dst_ref=view,
            send_sem=send,
            recv_sem=recv,
            device_id={"ctx": target},
            device_id_type=pl.DeviceIdType.MESH,
        )

    def to_right(k):
        return copy(at(1 - k, core), right, send_r.at[k - 1], recv_r.at[k - 1], 0 if k == 4 else None)

    def from_left(k):
        return copy(at(-k, core), right, send_r.at[k - 1], recv_r.at[k - 1], 0 if k == 4 else None)

    def to_left(k):
        return copy(at(k - 1, core), left, send_l.at[k - 1], recv_l.at[k - 1], 1 if k == 4 else None)

    def from_right(k):
        return copy(at(k, core), left, send_l.at[k - 1], recv_l.at[k - 1], 1 if k == 4 else None)

    def to_sibling(n, offset):
        return copy(at(offset, core), sibling, send_s.at[n], recv_s.at[n])

    def from_sibling(n, offset):
        return copy(at(offset, 1 - core), sibling, send_s.at[n], recv_s.at[n])

    order = [(0, 0), (-1, 0), (1, 0), (0, 1)]
    order += [(-2, 0), (2, 0), (-1, 1), (1, 1)]
    order += [(-3, 0), (3, 0), (-2, 1), (2, 1), (-3, 1), (3, 1), (4, 0), (4, 1)]
    number = {0: 0, -1: 1, 1: 2, -2: 3, 2: 4, -3: 5, 3: 6, 4: 7}

    def place(step):
        offset, other = order[step]
        return at(offset, 1 - core if other else core)

    def use(step):
        offset, other = order[step]
        if other:
            from_sibling(number[offset], offset).wait_recv()
        if consume is not None:
            consume(step, place(step), place(step + 1) if step + 1 < len(order) else None)

    to_right(1).start()
    to_left(1).start()
    to_sibling(0, 0).start()
    use(0)
    step = 1
    for k in (1, 2, 3):
        from_left(k).wait_recv()
        to_right(k + 1).start()
        to_sibling(number[-k], -k).start()
        from_right(k).wait_recv()
        to_left(k + 1).start()
        to_sibling(number[k], k).start()
        count = (3, 4, 6)[k - 1]
        for _ in range(count):
            use(step)
            step += 1
    from_left(4).wait_recv()
    from_right(4).wait_recv()
    to_sibling(7, 4).start()
    use(14)
    use(15)
    for k in (1, 2, 3, 4):
        to_right(k).wait_send()
        to_left(k).wait_send()
    for offset, n in number.items():
        to_sibling(n, offset).wait_send()


RING_SEMS = [
    pltpu.SemaphoreType.DMA,
    pltpu.SemaphoreType.DMA((4,)),
    pltpu.SemaphoreType.DMA((4,)),
    pltpu.SemaphoreType.DMA((4,)),
    pltpu.SemaphoreType.DMA((4,)),
    pltpu.SemaphoreType.DMA((8,)),
    pltpu.SemaphoreType.DMA((8,)),
]
VMEM_REF = pl.BlockSpec(memory_space=pltpu.VMEM)
ANY_REF = pl.BlockSpec(memory_space=pl.ANY)


def gather_kernel(x_ref, out_ref, *sems):
    ring_gather(x_ref, out_ref, sems)


def gathered_rows(x, collective_id):
    out = pl.pallas_call(
        gather_kernel,
        out_shape=jax.ShapeDtypeStruct((RING_SIZE,) + x.shape, x.dtype),
        in_specs=[ANY_REF],
        out_specs=ANY_REF,
        scratch_shapes=RING_SEMS,
        compiler_params=pltpu.CompilerParams(collective_id=collective_id, has_side_effects=True),
    )(x)
    return out.reshape((RING_SIZE * x.shape[0],) + x.shape[1:])


def weight_chunk(w_ref, wbuf, sem, origin, slot):
    depth = wbuf.shape[2]
    rows = pl.ds(pl.multiple_of(origin * depth, depth), depth)
    return pltpu.make_async_copy(w_ref.at[:, rows, :], wbuf.at[slot], sem.at[slot])


def hidden_kernel(width, x_ref, gain_ref, gate_ref, up_ref, out_ref, buf, wg, wu, ag, au, ss, wsem_g, wsem_u, *sems):
    experts = buf.shape[1]

    def fetch(origin, slot):
        weight_chunk(gate_ref, wg, wsem_g, origin, slot).start()
        weight_chunk(up_ref, wu, wsem_u, origin, slot).start()

    def consume(step, origin, following):
        slot = step % 2
        weight_chunk(gate_ref, wg, wsem_g, origin, slot).wait()
        weight_chunk(up_ref, wu, wsem_u, origin, slot).wait()
        if following is not None:
            fetch(following, 1 - slot)
        gain = gain_ref[origin]

        def one(e, carry):
            xf = buf[origin, e].astype(jnp.float32)
            xg = (xf * gain).astype(jnp.bfloat16)
            squares = jnp.sum(xf * xf, axis=-1, keepdims=True)
            g = jnp.dot(xg, wg[slot, e], preferred_element_type=jnp.float32)
            u = jnp.dot(xg, wu[slot, e], preferred_element_type=jnp.float32)
            if step == 0:
                ss[e] = squares
                ag[e] = g
                au[e] = u
            else:
                ss[e] += squares
                ag[e] += g
                au[e] += u
            return carry

        lax.fori_loop(0, experts, one, 0)

    ring_gather(x_ref, buf, sems, consume, lambda me: fetch(me, 0))

    def finish(e, carry):
        inverse = lax.rsqrt(ss[e] / width + 1e-05)
        g = ag[e] * inverse
        u = au[e] * inverse
        out_ref[e] = (g / (1.0 + jnp.exp(-g)) * u).astype(out_ref.dtype)
        return carry

    lax.fori_loop(0, experts, finish, 0)


def ring_hidden(rows, gain, gate_proj, up_proj):
    experts, count, depth = rows.shape
    units = gate_proj.shape[2]
    return pl.pallas_call(
        functools.partial(hidden_kernel, gate_proj.shape[1]),
        out_shape=jax.ShapeDtypeStruct((experts, count, units), jnp.bfloat16),
        in_specs=[ANY_REF, VMEM_REF, ANY_REF, ANY_REF],
        out_specs=VMEM_REF,
        scratch_shapes=[
            pltpu.VMEM((RING_SIZE, experts, count, depth), jnp.bfloat16),
            pltpu.VMEM((2, experts, depth, units), jnp.bfloat16),
            pltpu.VMEM((2, experts, depth, units), jnp.bfloat16),
            pltpu.VMEM((experts, count, units), jnp.float32),
            pltpu.VMEM((experts, count, units), jnp.float32),
            pltpu.VMEM((experts, count, 1), jnp.float32),
            pltpu.SemaphoreType.DMA((2,)),
            pltpu.SemaphoreType.DMA((2,)),
        ]
        + RING_SEMS,
        compiler_params=pltpu.CompilerParams(
            collective_id=2, has_side_effects=True, vmem_limit_bytes=48 * MIB
        ),
    )(rows, gain, gate_proj, up_proj)


def down_kernel(x_ref, down_ref, out_ref, buf, wd, wsem, *sems):
    experts = buf.shape[1]

    def consume(step, origin, following):
        slot = step % 2
        weight_chunk(down_ref, wd, wsem, origin, slot).wait()
        if following is not None:
            weight_chunk(down_ref, wd, wsem, following, 1 - slot).start()

        def one(e, carry):
            y = jnp.dot(buf[origin, e], wd[slot, e], preferred_element_type=jnp.float32)
            if step == 0:
                out_ref[e] = y
            else:
                out_ref[e] += y
            return carry

        lax.fori_loop(0, experts, one, 0)

    ring_gather(
        x_ref, buf, sems, consume, lambda me: weight_chunk(down_ref, wd, wsem, me, 0).start()
    )


def ring_down(hidden, down_proj):
    experts, count, depth = hidden.shape
    features = down_proj.shape[2]
    return pl.pallas_call(
        down_kernel,
        out_shape=jax.ShapeDtypeStruct((experts, count, features), jnp.float32),
        in_specs=[ANY_REF, ANY_REF],
        out_specs=VMEM_REF,
        scratch_shapes=[
            pltpu.VMEM((RING_SIZE, experts, count, depth), jnp.bfloat16),
            pltpu.VMEM((2, experts, depth, features), jnp.bfloat16),
            pltpu.SemaphoreType.DMA((2,)),
        ]
        + RING_SEMS,
        compiler_params=pltpu.CompilerParams(
            collective_id=3, has_side_effects=True, vmem_limit_bytes=48 * MIB
        ),
    )(hidden, down_proj)


def slot_ranks(expert_ids, n_experts, n_blocks):
    seq_len = expert_ids.shape[0]
    rows_block = seq_len // n_blocks
    labels = jnp.arange(n_experts, dtype=jnp.int32)
    onehot = (expert_ids[:, :, None] == labels[None, None, :]).astype(jnp.int32)
    hits = jnp.sum(onehot, axis=1).reshape(n_blocks, rows_block, n_experts)
    before = (jnp.cumsum(hits, axis=1) - hits).reshape(seq_len, n_experts)
    return jnp.sum(onehot * before[:, None, :], axis=2)


def on_device(
    ring,
    queries,
    projected_key_value,
    doc_ids,
    residual_in,
    out_proj,
    norm_gain,
    expert_ids,
    route_weights,
    gate_proj,
    up_proj,
    down_proj,
):
    def gather(x, collective_id):
        if ring:
            return gathered_rows(x, collective_id)
        return lax.all_gather(x, "ctx", axis=0, tiled=True)

    tok_count = queries.shape[0]
    head_groups = QUERY_HEADS // KEY_VALUE_HEADS
    kv_width = projected_key_value.shape[2]
    kv_local = kv_width // HEAD_WIDTH
    scale = 1.0 / math.sqrt(HEAD_WIDTH)
    heads_of_queries = queries.reshape(tok_count, kv_local, head_groups, HEAD_WIDTH)
    query_pos = lax.axis_index("ctx") * tok_count + jnp.arange(tok_count, dtype=jnp.int32)

    feat_local = norm_gain.shape[0]
    per_row = -(-feat_local // tok_count)
    gain_cols = jnp.pad(norm_gain, (0, per_row * tok_count - feat_local)).reshape(tok_count, per_row)
    side = jnp.concatenate([doc_ids.astype(jnp.bfloat16)[:, None], gain_cols], axis=1)
    side = jnp.pad(side, ((0, 0), (0, HEAD_WIDTH - 1 - per_row)))
    packed = jnp.concatenate([projected_key_value.reshape(tok_count, 2 * kv_width), side], axis=1)
    piece = gather(packed, 0)
    key_rows = piece.shape[0]
    ctx_size = key_rows // tok_count
    doc_piece = piece[:, 2 * kv_width].astype(jnp.int32)
    gain_piece = piece[:, 2 * kv_width + 1 : 2 * kv_width + 1 + per_row]
    gain_full = gain_piece.reshape(ctx_size, tok_count * per_row)[:, :feat_local].astype(jnp.float32)
    heads_of_keys = piece[:, :kv_width].reshape(key_rows, kv_local, HEAD_WIDTH)
    heads_of_values = piece[:, kv_width : 2 * kv_width].reshape(key_rows, kv_local, HEAD_WIDTH)
    key_pos = jnp.arange(key_rows, dtype=jnp.int32)
    visible = (doc_ids[:, None] == doc_piece[None, :]) & (key_pos[None, :] <= query_pos[:, None])
    scores = (
        jnp.einsum(
            "tkgd,skd->kgts", heads_of_queries, heads_of_keys, preferred_element_type=jnp.float32
        )
        * scale
    )
    scores = jnp.where(visible, scores, NEG)
    top = jnp.max(scores, axis=-1)
    expo = jnp.where(visible, jnp.exp(scores - top[..., None]), 0.0)
    total_new = jnp.sum(expo, axis=-1)
    weights = expo.astype(jnp.bfloat16)
    product = jnp.einsum(
        "kgts,skd->kgtd", weights, heads_of_values, preferred_element_type=jnp.float32
    )
    attended = (
        (product / total_new[..., None])
        .transpose(2, 0, 1, 3)
        .reshape(tok_count, -1)
        .astype(jnp.bfloat16)
    )
    partial_out = jnp.dot(gather(attended, 1), out_proj, preferred_element_type=jnp.float32)

    n_blocks = lax.axis_size("exp")
    block_index = lax.axis_index("exp")
    seq_len = expert_ids.shape[0]
    rows_block = seq_len // n_blocks
    capacity = rows_block * 9 // 32
    width = n_blocks * capacity
    local_experts = gate_proj.shape[0]
    rank = slot_ranks(expert_ids, EXPERTS, n_blocks)
    position = jnp.arange(seq_len, dtype=jnp.int32)
    slot_key = expert_ids * width + (position // rows_block)[:, None] * capacity + rank
    own_rows = lax.dynamic_slice_in_dim(
        partial_out, block_index * rows_block, rows_block, 0
    ) + residual_in.astype(jnp.float32)
    with_base = lax.dynamic_update_slice_in_dim(
        partial_out, own_rows, block_index * rows_block, 0
    ).astype(jnp.bfloat16)
    slots = jnp.arange(EXPERTS * width, dtype=jnp.int32)[:, None]
    chosen = ((slots == slot_key[None, :, 0]) | (slots == slot_key[None, :, 1])).astype(jnp.bfloat16)
    shares = jnp.dot(chosen, with_base, preferred_element_type=jnp.float32)
    received = lax.all_to_all(
        shares.astype(jnp.bfloat16).reshape(EXPERTS, width, feat_local),
        "exp",
        split_axis=0,
        concat_axis=1,
        tiled=True,
    ).astype(jnp.float32)
    expert_rows = jnp.sum(
        received.reshape(local_experts, n_blocks, -1, feat_local), axis=1
    ).astype(jnp.bfloat16)

    my_slots = block_index * local_experts * width + jnp.arange(local_experts * width, dtype=jnp.int32)
    lead = my_slots[:, None] == slot_key[None, :, 0]
    second = my_slots[:, None] == slot_key[None, :, 1]
    my_weight = jnp.sum(
        jnp.where(lead, route_weights[None, :, 0], jnp.where(second, route_weights[None, :, 1], 0.0)),
        axis=1,
    ).reshape(local_experts, width)
    my_first = jnp.sum(lead.astype(jnp.float32), axis=1).reshape(local_experts, width)

    if ring:
        hidden = ring_hidden(expert_rows, gain_full[:, None, :], gate_proj, up_proj)
        expert_out = ring_down(hidden, down_proj)
    else:
        full_rows = lax.all_gather(expert_rows, "ctx", axis=2, tiled=True)
        meansq = (
            jnp.einsum("erd,erd->er", full_rows, full_rows, preferred_element_type=jnp.float32)
            / full_rows.shape[2]
        )
        inverse = lax.rsqrt(meansq + 1e-05)
        normed = (
            full_rows.astype(jnp.float32) * inverse[..., None] * gain_full.reshape(-1)
        ).astype(jnp.bfloat16)
        gate = jnp.einsum("erd,edf->erf", normed, gate_proj, preferred_element_type=jnp.float32)
        upper = jnp.einsum("erd,edf->erf", normed, up_proj, preferred_element_type=jnp.float32)
        hidden = (jax.nn.silu(gate) * upper).astype(jnp.bfloat16)
        expert_out = jnp.einsum(
            "erf,efd->erd",
            lax.all_gather(hidden, "ctx", axis=2, tiled=True),
            down_proj,
            preferred_element_type=jnp.float32,
        )
    payload = my_weight[..., None] * expert_out + my_first[..., None] * expert_rows.astype(
        jnp.float32
    )
    back = lax.all_to_all(
        payload.reshape(local_experts, n_blocks, capacity, feat_local).astype(jnp.bfloat16),
        "exp",
        split_axis=1,
        concat_axis=0,
        tiled=True,
    )
    back = back.reshape(EXPERTS * capacity, feat_local)
    block_key = lax.dynamic_slice_in_dim(
        expert_ids * capacity + rank, block_index * rows_block, rows_block, 0
    )
    labels = jnp.arange(EXPERTS * capacity, dtype=jnp.int32)[None, :]
    picker = ((labels == block_key[:, :1]) | (labels == block_key[:, 1:])).astype(jnp.bfloat16)
    mixed = jnp.dot(picker, back, preferred_element_type=jnp.float32)
    return mixed.astype(jnp.bfloat16)


def solution(mesh):
    ring = mesh.shape["ctx"] == RING_SIZE
    placed = (
        P("ctx", "exp"),
        P("ctx", None, "exp"),
        P("ctx"),
        P("exp", "ctx"),
        P("exp", "ctx"),
        P("ctx"),
        P(),
        P(),
        P("exp", None, "ctx"),
        P("exp", None, "ctx"),
        P("exp", None, "ctx"),
    )
    return jax.shard_map(
        functools.partial(on_device, ring),
        mesh=mesh,
        in_specs=placed,
        out_specs=P("exp", "ctx"),
        check_vma=False,
    )
```

time: 490 us -> 343 us (0.70)
  Pallas kernels: 0 us -> 257 us
  waiting for transfers between devices: 275 us -> 31.6 us
  matrix products: 71.8 us -> 19.5 us
  local copies, waits for them, and re-layouts: 65.6 us -> 15 us
  blocking collectives: 33.2 us -> 0 us
  between operations: 14.2 us -> 0.26 us
  other arithmetic: 21.6 us -> 10.3 us
    pallas_call x0 -> x4, Pallas kernels: none -> 257 us  [the longest x1 98.6 us: ring_down(): pl.pallas_call(down_kernel, out_shape=jax.ShapeDtypeStruct((experts, coun...]
    all_gather x4 -> x0, waiting for transfers between devices: 241 us -> none  [the longest x1 92.2 us: on_device(): lax.all_gather(expert_rows, 'ctx', axis=2, tiled=True)]
    dot_general x6 -> x3, matrix products: 70.1 us -> 10.9 us  [the longest x1 5.53 us: on_device(): jnp.dot(gather(attended, 1), out_proj, preferred_element_type=jnp.float32)]
    unnamed x51 -> x19, local copies, waits for them, and re-layouts: 43 us -> 5.79 us
    all_gather x1 -> x0, blocking collectives: 19.5 us -> none  [on_device(): lax.all_gather(norm_gain, 'ctx', axis=0, tiled=True)]
    unnamed x1 -> x0, blocking collectives: 13.7 us -> none
    gather x1 -> x0, local copies, waits for them, and re-layouts: 7.97 us -> none  [on_device(): shares = jnp.take(with_base, tok_of, axis=0) * valid[..., None]]
    dot_general x1 -> x0, other arithmetic: 7.84 us -> none  [on_device(): jnp.einsum('erd,erd->er', full_rows, full_rows, preferred_element_type=jn...]
  transfers between devices with their start and end apart: 6 -> 2, of which waited for: 6 -> 2; matrix products, arithmetic and copies ran while one was open for 9% -> 1% of each run, Pallas kernels for 0% -> 0%
where the time goes in v1:
time: 343 us; the launch traced here: 342 us
  Pallas kernels  257 us (75%)
  waiting for transfers between devices  31.6 us (9%)
  matrix products  19.5 us (6%)
  local copies, waits for them, and re-layouts  15 us (4%)
  other arithmetic  10.3 us (3%)
  starting transfers between devices  7.7 us (2%)
    pallas_call x1, Pallas kernels, ring_down(): pl.pallas_call(down_kernel, out_shape=jax.ShapeDtypeStruct((experts, coun...  98.6 us
    pallas_call x2, Pallas kernels, gathered_rows(): pl.pallas_call(gather_kernel, out_shape=jax.ShapeDtypeStruct((RING_SIZE,)...  80.6 us
    pallas_call x1, Pallas kernels, ring_hidden(): pl.pallas_call(functools.partial(hidden_kernel, gate_proj.shape[1]), out_...  78 us
    all_to_all x1, waiting for transfers between devices, on_device(): lax.all_to_all(shares.astype(jnp.bfloat16).reshape(EXPERTS, width, feat_l...  18.8 us
    all_to_all x1, waiting for transfers between devices, on_device(): lax.all_to_all(payload.reshape(local_experts, n_blocks, capacity, feat_lo...  12.8 us
  transfers between devices with their start and end apart: 2, of which 2 were waited for; matrix products, arithmetic and copies ran while one was open for 1% of the time, Pallas kernels for 0%

profile of v1, /device:TPU:0, one launch (start us, length us, event | category | flops | bytes accessed | tf_op | source)
XLA Modules:
  0.0 341.6 jit_solution(10144270918723353265)
XLA Ops:
  0.0 0.0 copy-start
  0.0 0.8 convert_bitcast_fusion
  0.8 0.1 copy.49
  0.9 0.8 reshape.104
  1.8 0.9 copy.66
  2.7 0.1 fusion.47
  2.8 0.7 pad_maximum_fusion.x_ref
  3.4 29.2 %shard_map.109 = bf16[16,64,1152]{2,1,0:T(8,128)(2,1)} custom-call(bf16[64,1152]{1,0:T(8,128)(2,1)} %pad_maximum_fusion.x_ref), custom_call_target="tpu_custom_call" | custom-call | tf_op jit(solution)/shard_map/pallas_call | solution.py:152
  32.7 0.0 copy-start.5
  32.7 1.2 convert_reduce_fusion
  33.9 2.7 fusion.54
  36.5 0.0 copy-done.5
  36.6 2.3 reduce-window.6
  38.8 0.3 slice_reduce_fusion
  39.2 0.1 bitcast_subtract_fusion
  39.3 0.0 copy-start.7
  39.3 2.3 reshape.107
  41.6 2.3 copy.64
  43.9 1.3 copy.65
  45.2 0.1 fusion.44
  45.4 5.7 %fusion.58 = (f32[4,6,64]{2,1,0:T(8,128)S(1)}, bf16[4,6,64,1024]{3,2,1,0:T(8,128)(2,1)}) fusion(bf16[1024,4,128,1]{0,2,3,1:T(8,128)(2,1)} %bitcast.73, pred[64,1024]{1,0:T(8,128)(4,1)S(1)} %fusion.44, bf16[64,4,6,128]{3,2,1,0:T(8,128)(2,1)} %reshape.107), kind=kOutput, calls=%fused_computation.71 | convolution fusion | flops 412091392 | bytes 4659200 | tf_op jit(solution)/shard_map/sub | solution.py:344
  51.0 2.9 fusion.28
  53.9 0.3 copy.55
  54.2 1.2 convert_element_type.74.x_ref
  55.4 51.4 %shard_map.110 = bf16[16,64,3072]{2,1,0:T(8,128)(2,1)} custom-call(bf16[64,3072]{1,0:T(8,128)(2,1)} %convert_element_type.74.x_ref), custom_call_target="tpu_custom_call" | custom-call | tf_op jit(solution)/shard_map/pallas_call | solution.py:152
  106.8 0.0 copy-start.4
  106.8 5.5 %fusion.63 = f32[1024,384]{1,0:T(8,128)S(1)} fusion(bf16[1024,3072]{1,0:T(8,128)(2,1)} %bitcast.69, bf16[3072,384]{1,0:T(8,128)(2,1)S(1)} %copy-done), kind=kOutput, calls=%fused_computation.72 | convolution fusion | flops 2415919104 | bytes 10223616 | tf_op jit(solution)/shard_map/dot_general | solution.py:356
  112.4 0.1 add_dynamic-update-slice_fusion
  112.5 3.8 %fusion.9 = bf16[2304,384]{1,0:T(8,128)(2,1)} fusion(s32[1024]{0:T(1024)S(1)} %bitcast.82, s32[1024]{0:T(1024)S(1)} %bitcast.80, f32[1024,384]{1,0:T(8,128)S(1)} %add_dynamic-update-slice_fusion), kind=kOutput, calls=%fused_computation.14 | convolution fusion | flops 1820295168 | bytes 3350528 | tf_op jit(solution)/shard_map/dot_general | solution.py:376
  116.3 4.0 %all-to-all-start = ((bf16[8,288,384]{2,1,0:T(8,128)(2,1)}), bf16[8,288,384]{2,1,0:T(8,128)(2,1)S(1)}, u32[]{:S(2)}, u32[]{:S(2)}) async-start(bf16[8,288,384]{2,1,0:T(8,128)(2,1)} %bitcast.71), calls=%async_computation | async-start | bytes 3538944 | tf_op jit(solution)/shard_map/all_to_all | solution.py:377
  120.3 0.0 copy-done.6
  120.4 1.5 fusion.5
  121.9 0.1 mul.85
  121.9 0.1 mul.92
  122.0 1.1 slice_convert_fusion
  123.1 0.4 reshape.116.gain_ref
  123.5 18.8 %all-to-all-done = bf16[8,288,384]{2,1,0:T(8,128)(2,1)S(1)} async-done(((bf16[8,288,384]{2,1,0:T(8,128)(2,1)}), bf16[8,288,384]{2,1,0:T(8,128)(2,1)S(1)}, u32[]{:S(2)}, u32[]{:S(2)}) %all-to-all-start) | async-done | bytes 1769504 | tf_op jit(solution)/shard_map/all_to_all | solution.py:377
  142.3 1.2 copy-done.2
  143.5 1.9 reduce_sum.61.x_ref
  145.4 78.0 %shard_map.111.x_ref = bf16[4,288,512]{2,1,0:T(8,128)(2,1)S(1)} custom-call(bf16[4,288,384]{2,1,0:T(8,128)(2,1)S(1)} %reduce_sum.61.x_ref, f32[16,1,384]{2,1,0:T(1,128)S(1)} %reshape.116.gain_ref, bf16[4,6144,512]{2,1,0:T(8,128)(2,1)} %gate_ref.1, bf16[4,6144,512]{2,1,0:T(8,128)(2,1)} %up_ref.1), custom_call_target="tpu_custom_call" | custom-call | tf_op jit(solution)/shard_map/pallas_call | solution.py:217
  223.5 98.6 %shard_map.112 = f32[4,288,384]{2,1,0:T(8,128)S(1)} custom-call(bf16[4,288,512]{2,1,0:T(8,128)(2,1)S(1)} %shard_map.111.x_ref, bf16[4,8192,384]{2,1,0:T(8,128)(2,1)} %down_ref.1), custom_call_target="tpu_custom_call" | custom-call | tf_op jit(solution)/shard_map/pallas_call | solution.py:266
  322.1 0.4 add_convert_fusion
  322.4 0.0 copy-start.1
  322.5 1.0 copy.57
  323.5 3.7 %all-to-all-start.1 = ((bf16[4,2,144,384]{3,2,0,1:T(8,128)(2,1)}), bf16[4,2,144,384]{3,2,0,1:T(8,128)(2,1)S(1)}, u32[]{:S(2)}, u32[]{:S(2)}) async-start(bf16[4,2,144,384]{3,2,0,1:T(8,128)(2,1)} %copy.57), calls=%async_computation.1 | async-start | bytes 1769472 | tf_op jit(solution)/shard_map/all_to_all | solution.py:422
  327.2 12.8 %all-to-all-done.1 = bf16[4,2,144,384]{3,2,0,1:T(8,128)(2,1)S(1)} async-done(((bf16[4,2,144,384]{3,2,0,1:T(8,128)(2,1)}), bf16[4,2,144,384]{3,2,0,1:T(8,128)(2,1)S(1)}, u32[]{:S(2)}, u32[]{:S(2)}) %all-to-all-start.1) | async-done | bytes 884768 | tf_op jit(solution)/shard_map/all_to_all | solution.py:422
  340.0 1.6 fusion.31
  341.6 0.0 copy-done.1
  (19 shorter events, 0.2 us)
Async XLA Ops:
  0.0 106.8 %copy-start = (bf16[3072,384]{1,0:T(8,128)(2,1)S(1)}, bf16[3072,384]{1,0:T(8,128)(2,1)}, u32[]{:S(2)}) copy-start(bf16[3072,384]{1,0:T(8,128)(2,1)} %param.15) | copy-start | bytes 7077892
  32.7 3.9 %copy-start.5 = (s32[1024,2]{0,1:T(2,128)S(1)}, s32[1024,2]{0,1:T(2,128)}, u32[]{:S(2)}) copy-start(s32[1024,2]{0,1:T(2,128)} %param.17) | copy-start | bytes 24580
  39.3 5.9 %copy-start.7 = (s32[64]{0:T(128)S(1)}, s32[64]{0:T(128)}, u32[]{:S(2)}) copy-start(s32[64]{0:T(128)} %param.13) | copy-start | bytes 772
  45.4 5.7 %copy-start.3 = (bf16[1024,512]{0,1:T(8,128)(2,1)S(1)}, bf16[1024,512]{0,1:T(8,128)(2,1)}, u32[]{:S(2)}) copy-start(bf16[1024,512]{0,1:T(8,128)(2,1)} %copy.65) | copy-start | bytes 3145732
  106.8 5.6 %copy-start.4 = (bf16[512,384]{1,0:T(8,128)(2,1)S(1)}, bf16[512,384]{1,0:T(8,128)(2,1)}, u32[]{:S(2)}) copy-start(bf16[512,384]{1,0:T(8,128)(2,1)} %param.14) | copy-start | bytes 1179652
  116.3 4.0 %copy-start.6 = (f32[1024,2]{0,1:T(2,128)S(1)}, f32[1024,2]{0,1:T(2,128)}, u32[]{:S(2)}) copy-start(f32[1024,2]{0,1:T(2,128)} %param.18) | copy-start | bytes 24580
  116.3 26.0 %all-to-all-start = ((bf16[8,288,384]{2,1,0:T(8,128)(2,1)}), bf16[8,288,384]{2,1,0:T(8,128)(2,1)S(1)}, u32[]{:S(2)}, u32[]{:S(2)}) async-start(bf16[8,288,384]{2,1,0:T(8,128)(2,1)} %bitcast.71), calls=%async_computation | async-start | bytes 3538944 | tf_op jit(solution)/shard_map/all_to_all | solution.py:377
  142.3 1.2 copy-start.2
  322.4 19.2 %copy-start.1 = (bf16[3072,384]{1,0:T(8,128)(2,1)S(1)}, bf16[3072,384]{1,0:T(8,128)(2,1)}, u32[]{:S(2)}) copy-start(bf16[3072,384]{1,0:T(8,128)(2,1)} %param.15) | copy-start | bytes 7077892
  323.5 16.5 %all-to-all-start.1 = ((bf16[4,2,144,384]{3,2,0,1:T(8,128)(2,1)}), bf16[4,2,144,384]{3,2,0,1:T(8,128)(2,1)S(1)}, u32[]{:S(2)}, u32[]{:S(2)}) async-start(bf16[4,2,144,384]{3,2,0,1:T(8,128)(2,1)} %copy.57), calls=%async_computation.1 | async-start | bytes 1769472 | tf_op jit(solution)/shard_map/all_to_all | solution.py:422

commit v2 on v1

--- a/solution.py
+++ b/solution.py
@@ -69,17 +69,13 @@
             device_id_type=pl.DeviceIdType.MESH,
         )
 
-    def to_right(k):
-        return copy(at(1 - k, core), right, send_r.at[k - 1], recv_r.at[k - 1], 0 if k == 4 else None)
-
-    def from_left(k):
-        return copy(at(-k, core), right, send_r.at[k - 1], recv_r.at[k - 1], 0 if k == 4 else None)
-
-    def to_left(k):
-        return copy(at(k - 1, core), left, send_l.at[k - 1], recv_l.at[k - 1], 1 if k == 4 else None)
-
-    def from_right(k):
-        return copy(at(k, core), left, send_l.at[k - 1], recv_l.at[k - 1], 1 if k == 4 else None)
+    def rightward(k, part, sent):
+        n = 2 * (k - 1) + part
+        return copy(at(1 - k if sent else -k, core), right, send_r.at[n], recv_r.at[n], part)
+
+    def leftward(k, part, sent):
+        n = 2 * (k - 1) + part
+        return copy(at(k - 1 if sent else k, core), left, send_l.at[n], recv_l.at[n], part)
 
     def to_sibling(n, offset):
         return copy(at(offset, core), sibling, send_s.at[n], recv_s.at[n])
@@ -103,40 +99,53 @@
         if consume is not None:
             consume(step, place(step), place(step + 1) if step + 1 < len(order) else None)
 
-    to_right(1).start()
-    to_left(1).start()
+    rightward(1, 0, True).start()
+    leftward(1, 1, True).start()
+    rightward(1, 1, True).start()
+    leftward(1, 0, True).start()
     to_sibling(0, 0).start()
-    use(0)
-    step = 1
+    before = {1: (0,), 2: (1, 2), 3: (4, 5)}
+    between = {1: (), 2: (3,), 3: (6, 7)}
     for k in (1, 2, 3):
-        from_left(k).wait_recv()
-        to_right(k + 1).start()
+        for step in before[k]:
+            use(step)
+        rightward(k, 0, False).wait_recv()
+        rightward(k + 1, 0, True).start()
+        leftward(k, 1, False).wait_recv()
+        leftward(k + 1, 1, True).start()
+        for step in between[k]:
+            use(step)
+        rightward(k, 1, False).wait_recv()
+        if k < 3:
+            rightward(k + 1, 1, True).start()
         to_sibling(number[-k], -k).start()
-        from_right(k).wait_recv()
-        to_left(k + 1).start()
+        leftward(k, 0, False).wait_recv()
+        if k < 3:
+            leftward(k + 1, 0, True).start()
         to_sibling(number[k], k).start()
-        count = (3, 4, 6)[k - 1]
-        for _ in range(count):
-            use(step)
-            step += 1
-    from_left(4).wait_recv()
-    from_right(4).wait_recv()
+    for step in (8, 9, 10, 11):
+        use(step)
+    rightward(4, 0, False).wait_recv()
+    leftward(4, 1, False).wait_recv()
     to_sibling(7, 4).start()
-    use(14)
-    use(15)
+    for step in (12, 13, 14, 15):
+        use(step)
     for k in (1, 2, 3, 4):
-        to_right(k).wait_send()
-        to_left(k).wait_send()
+        rightward(k, 0, True).wait_send()
+        leftward(k, 1, True).wait_send()
+        if k < 4:
+            rightward(k, 1, True).wait_send()
+            leftward(k, 0, True).wait_send()
     for offset, n in number.items():
         to_sibling(n, offset).wait_send()
 
 
 RING_SEMS = [
     pltpu.SemaphoreType.DMA,
-    pltpu.SemaphoreType.DMA((4,)),
-    pltpu.SemaphoreType.DMA((4,)),
-    pltpu.SemaphoreType.DMA((4,)),
-    pltpu.SemaphoreType.DMA((4,)),
+    pltpu.SemaphoreType.DMA((8,)),
+    pltpu.SemaphoreType.DMA((8,)),
+    pltpu.SemaphoreType.DMA((8,)),
+    pltpu.SemaphoreType.DMA((8,)),
     pltpu.SemaphoreType.DMA((8,)),
     pltpu.SemaphoreType.DMA((8,)),
 ]
@@ -148,16 +157,72 @@
     ring_gather(x_ref, out_ref, sems)
 
 
-def gathered_rows(x, collective_id):
+def gathered_rows(x):
     out = pl.pallas_call(
         gather_kernel,
         out_shape=jax.ShapeDtypeStruct((RING_SIZE,) + x.shape, x.dtype),
         in_specs=[ANY_REF],
-        out_specs=ANY_REF,
+        out_specs=VMEM_REF,
         scratch_shapes=RING_SEMS,
-        compiler_params=pltpu.CompilerParams(collective_id=collective_id, has_side_effects=True),
+        compiler_params=pltpu.CompilerParams(
+            collective_id=0, has_side_effects=True, vmem_limit_bytes=16 * MIB
+        ),
     )(x)
     return out.reshape((RING_SIZE * x.shape[0],) + x.shape[1:])
+
+
+def project_kernel(x_ref, w_ref, out_ref, buf, *sems):
+    ring_gather(x_ref, buf, sems)
+    shards = 4
+    rows = shards * x_ref.shape[0]
+    for group in range(RING_SIZE // shards):
+        x = buf[pl.ds(group * shards, shards)].reshape(rows, x_ref.shape[1])
+        out_ref[pl.ds(group * rows, rows), :] = jnp.dot(
+            x, w_ref[...], preferred_element_type=jnp.float32
+        )
+
+
+def ring_project(x, weight):
+    return pl.pallas_call(
+        project_kernel,
+        out_shape=jax.ShapeDtypeStruct((RING_SIZE * x.shape[0], weight.shape[1]), jnp.float32),
+        in_specs=[ANY_REF, VMEM_REF],
+        out_specs=VMEM_REF,
+        scratch_shapes=[pltpu.VMEM((RING_SIZE,) + x.shape, x.dtype)] + RING_SEMS,
+        compiler_params=pltpu.CompilerParams(
+            collective_id=1, has_side_effects=True, vmem_limit_bytes=40 * MIB
+        ),
+    )(x, weight)
+
+
+def attention_kernel(scale, q_ref, kv_ref, bias_ref, out_ref):
+    count, width = q_ref.shape[0], HEAD_WIDTH
+    group = QUERY_HEADS // KEY_VALUE_HEADS
+    heads = q_ref.shape[1] // (group * width)
+    bias = bias_ref[...]
+    for h in range(heads):
+        k = kv_ref[:, h * width : (h + 1) * width]
+        v = kv_ref[:, (heads + h) * width : (heads + h + 1) * width]
+        for g in range(h * group, (h + 1) * group):
+            cols = slice(g * width, (g + 1) * width)
+            scores = lax.dot_general(
+                q_ref[:, cols], k, (((1,), (1,)), ((), ())), preferred_element_type=jnp.float32
+            )
+            scores = scores * scale + bias
+            expo = jnp.exp(scores - jnp.max(scores, axis=-1, keepdims=True))
+            total = jnp.sum(expo, axis=-1, keepdims=True)
+            product = jnp.dot(expo.astype(jnp.bfloat16), v, preferred_element_type=jnp.float32)
+            out_ref[:, cols] = (product / total).astype(jnp.bfloat16)
+
+
+def local_attention(scale, queries, piece, visible):
+    return pl.pallas_call(
+        functools.partial(attention_kernel, scale),
+        out_shape=jax.ShapeDtypeStruct(queries.shape, jnp.bfloat16),
+        in_specs=[VMEM_REF] * 3,
+        out_specs=VMEM_REF,
+        compiler_params=pltpu.CompilerParams(vmem_limit_bytes=40 * MIB),
+    )(queries, piece, jnp.where(visible, 0.0, NEG))
 
 
 def weight_chunk(w_ref, wbuf, sem, origin, slot):
@@ -304,11 +369,6 @@
     up_proj,
     down_proj,
 ):
-    def gather(x, collective_id):
-        if ring:
-            return gathered_rows(x, collective_id)
-        return lax.all_gather(x, "ctx", axis=0, tiled=True)
-
     tok_count = queries.shape[0]
     head_groups = QUERY_HEADS // KEY_VALUE_HEADS
     kv_width = projected_key_value.shape[2]
@@ -323,7 +383,7 @@
     side = jnp.concatenate([doc_ids.astype(jnp.bfloat16)[:, None], gain_cols], axis=1)
     side = jnp.pad(side, ((0, 0), (0, HEAD_WIDTH - 1 - per_row)))
     packed = jnp.concatenate([projected_key_value.reshape(tok_count, 2 * kv_width), side], axis=1)
-    piece = gather(packed, 0)
+    piece = gathered_rows(packed) if ring else lax.all_gather(packed, "ctx", axis=0, tiled=True)
     key_rows = piece.shape[0]
     ctx_size = key_rows // tok_count
     doc_piece = piece[:, 2 * kv_width].astype(jnp.int32)
@@ -333,27 +393,35 @@
     heads_of_values = piece[:, kv_width : 2 * kv_width].reshape(key_rows, kv_local, HEAD_WIDTH)
     key_pos = jnp.arange(key_rows, dtype=jnp.int32)
     visible = (doc_ids[:, None] == doc_piece[None, :]) & (key_pos[None, :] <= query_pos[:, None])
-    scores = (
-        jnp.einsum(
-            "tkgd,skd->kgts", heads_of_queries, heads_of_keys, preferred_element_type=jnp.float32
-        )
-        * scale
-    )
-    scores = jnp.where(visible, scores, NEG)
-    top = jnp.max(scores, axis=-1)
-    expo = jnp.where(visible, jnp.exp(scores - top[..., None]), 0.0)
-    total_new = jnp.sum(expo, axis=-1)
-    weights = expo.astype(jnp.bfloat16)
-    product = jnp.einsum(
-        "kgts,skd->kgtd", weights, heads_of_values, preferred_element_type=jnp.float32
-    )
-    attended = (
-        (product / total_new[..., None])
-        .transpose(2, 0, 1, 3)
-        .reshape(tok_count, -1)
-        .astype(jnp.bfloat16)
-    )
-    partial_out = jnp.dot(gather(attended, 1), out_proj, preferred_element_type=jnp.float32)
+    if ring:
+        attended = local_attention(scale, queries, piece, visible)
+        partial_out = ring_project(attended, out_proj)
+    else:
+        scores = (
+            jnp.einsum(
+                "tkgd,skd->kgts", heads_of_queries, heads_of_keys, preferred_element_type=jnp.float32
+            )
+            * scale
+        )
+        scores = jnp.where(visible, scores, NEG)
+        top = jnp.max(scores, axis=-1)
+        expo = jnp.where(visible, jnp.exp(scores - top[..., None]), 0.0)
+        total_new = jnp.sum(expo, axis=-1)
+        weights = expo.astype(jnp.bfloat16)
+        product = jnp.einsum(
+            "kgts,skd->kgtd", weights, heads_of_values, preferred_element_type=jnp.float32
+        )
+        attended = (
+            (product / total_new[..., None])
+            .transpose(2, 0, 1, 3)
+            .reshape(tok_count, -1)
+            .astype(jnp.bfloat16)
+        )
+        partial_out = jnp.dot(
+            lax.all_gather(attended, "ctx", axis=0, tiled=True),
+            out_proj,
+            preferred_element_type=jnp.float32,
+        )
 
     n_blocks = lax.axis_size("exp")
     block_index = lax.axis_index("exp")

time: 343 us -> 302 us (0.88)
  matrix products: 19.5 us -> 5.4 us
  Pallas kernels: 257 us -> 243 us
  local copies, waits for them, and re-layouts: 15 us -> 3.75 us
    pallas_call x2 -> x1, Pallas kernels: 80.6 us -> 21.2 us  [gathered_rows(): pl.pallas_call(gather_kernel, out_shape=jax.ShapeDtypeStruct((RING_SIZE,)...]
    pallas_call x0 -> x2, Pallas kernels: none -> 46.1 us  [the longest x1 38 us: ring_project(): pl.pallas_call(project_kernel, out_shape=jax.ShapeDtypeStruct((RING_SIZE...]
    dot_general x2 -> x0, matrix products: 8.4 us -> none  [the longest x1 5.53 us: on_device(): jnp.dot(gather(attended, 1), out_proj, preferred_element_type=jnp.float32)]
    sub x1 -> x0, matrix products: 5.67 us -> none  [on_device(): expo = jnp.where(visible, jnp.exp(scores - top[..., None]), 0.0)]
    unnamed x19 -> x13, local copies, waits for them, and re-layouts: 5.79 us -> 0.95 us
where the time goes in v2:
time: 302 us
  Pallas kernels  243 us (80%)
  waiting for transfers between devices  30.8 us (10%)
  other arithmetic  9.77 us (3%)
  starting transfers between devices  8.55 us (3%)
  matrix products  5.4 us (2%)
  local copies, waits for them, and re-layouts  3.75 us (1%)
    pallas_call x1, Pallas kernels, ring_down(): pl.pallas_call(down_kernel, out_shape=jax.ShapeDtypeStruct((experts, coun...  97 us
    pallas_call x1, Pallas kernels, ring_hidden(): pl.pallas_call(functools.partial(hidden_kernel, gate_proj.shape[1]), out_...  78.6 us
    pallas_call x1, Pallas kernels, ring_project(): pl.pallas_call(project_kernel, out_shape=jax.ShapeDtypeStruct((RING_SIZE...  38 us
    pallas_call x1, Pallas kernels, gathered_rows(): pl.pallas_call(gather_kernel, out_shape=jax.ShapeDtypeStruct((RING_SIZE,)...  21.2 us
    all_to_all x1, waiting for transfers between devices, on_device(): lax.all_to_all(shares.astype(jnp.bfloat16).reshape(EXPERTS, width, feat_l...  19.9 us
    all_to_all x1, waiting for transfers between devices, on_device(): lax.all_to_all(payload.reshape(local_experts, n_blocks, capacity, feat_lo...  11 us
    pallas_call x1, Pallas kernels, local_attention(): pl.pallas_call(functools.partial(attention_kernel, scale), out_shape=jax....  8.1 us
  transfers between devices with their start and end apart: 2, of which 2 were waited for; matrix products, arithmetic and copies ran while one was open for 1% of the time, Pallas kernels for 0%

profile of v2, /device:TPU:0, one launch (start us, length us, event | category | flops | bytes accessed | tf_op | source)
XLA Modules:
  0.0 301.6 jit_solution(6335987999162486034)
XLA Ops:
  0.0 0.0 copy-start.5
  0.0 0.0 copy-start.1
  0.0 0.7 convert_bitcast_fusion
  0.7 0.1 copy.29
  0.8 0.8 reshape.88
  1.7 0.7 convert_reduce_fusion.1
  2.4 2.3 reduce-window.6
  4.7 0.3 slice_reduce_fusion
  5.0 0.1 bitcast_subtract_fusion
  5.1 0.7 select_reduce_fusion
  5.8 0.7 add_add_fusion
  6.5 0.9 copy.32
  7.5 0.1 fusion.23
  7.6 21.2 %shard_map.109 = bf16[16,64,1152]{2,1,0:T(8,128)(2,1)S(1)} custom-call(bf16[64,1152]{1,0:T(8,128)(2,1)S(1)} %pad_maximum_fusion.x_ref), custom_call_target="tpu_custom_call" | custom-call | tf_op jit(solution)/shard_map/pallas_call | solution.py:161
  28.8 0.2 convert_reduce_fusion
  29.0 0.0 copy-done.5
  29.0 0.0 copy-start
  29.1 0.1 fusion.20.bias_ref
  29.2 0.0 copy-done.1
  29.2 8.1 %shard_map.110.x_ref = bf16[64,3072]{1,0:T(8,128)(2,1)S(1)} custom-call(bf16[64,3072]{1,0:T(8,128)(2,1)S(1)} %copy-done.1, bf16[1024,1152]{1,0:T(8,128)(2,1)S(1)} %bitcast.31, f32[64,1024]{1,0:T(8,128)S(1)} %fusion.20.bias_ref), custom_call_target="tpu_custom_call" | custom-call | tf_op jit(solution)/shard_map/pallas_call | solution.py:219
  37.3 0.0 copy-done
  37.3 0.0 copy-start.2
  37.3 38.0 %shard_map.111 = f32[1024,384]{1,0:T(8,128)S(1)} custom-call(bf16[64,3072]{1,0:T(8,128)(2,1)S(1)} %shard_map.110.x_ref, bf16[3072,384]{1,0:T(8,128)(2,1)S(1)} %copy-done), custom_call_target="tpu_custom_call" | custom-call | tf_op jit(solution)/shard_map/pallas_call | solution.py:186
  75.3 0.0 copy-done.2
  75.3 0.1 add_dynamic-update-slice_fusion
  75.5 3.8 %fusion.7 = bf16[2304,384]{1,0:T(8,128)(2,1)} fusion(s32[1024]{0:T(1024)S(1)} %bitcast.43, s32[1024]{0:T(1024)S(1)} %bitcast.41, f32[1024,384]{1,0:T(8,128)S(1)} %add_dynamic-update-slice_fusion), kind=kOutput, calls=%fused_computation.10 | convolution fusion | flops 1820295168 | bytes 3350528 | tf_op jit(solution)/shard_map/dot_general | solution.py:444
  79.3 0.0 copy-start.4
  79.3 5.0 %all-to-all-start = ((bf16[8,288,384]{2,1,0:T(8,128)(2,1)}), bf16[8,288,384]{2,1,0:T(8,128)(2,1)}, u32[]{:S(2)}, u32[]{:S(2)}) async-start(bf16[8,288,384]{2,1,0:T(8,128)(2,1)} %bitcast.34), calls=%async_computation | async-start | bytes 3538944 | tf_op jit(solution)/shard_map/all_to_all | solution.py:445
  84.3 0.0 copy-done.4
  84.3 1.5 fusion.3
  85.8 0.1 mul.76
  85.9 0.1 mul.80
  86.0 0.1 slice_convert_fusion
  86.1 0.4 reshape.94.gain_ref
  86.5 19.9 %all-to-all-done = bf16[8,288,384]{2,1,0:T(8,128)(2,1)} async-done(((bf16[8,288,384]{2,1,0:T(8,128)(2,1)}), bf16[8,288,384]{2,1,0:T(8,128)(2,1)}, u32[]{:S(2)}, u32[]{:S(2)}) %all-to-all-start) | async-done | bytes 1769504 | tf_op jit(solution)/shard_map/all_to_all | solution.py:445
  106.4 1.9 reduce_sum.51.x_ref
  108.3 78.6 %shard_map.112.x_ref = bf16[4,288,512]{2,1,0:T(8,128)(2,1)S(1)} custom-call(bf16[4,288,384]{2,1,0:T(8,128)(2,1)S(1)} %reduce_sum.51.x_ref, f32[16,1,384]{2,1,0:T(1,128)S(1)} %reshape.94.gain_ref, bf16[4,6144,512]{2,1,0:T(8,128)(2,1)} %gate_ref.1, bf16[4,6144,512]{2,1,0:T(8,128)(2,1)} %up_ref.1), custom_call_target="tpu_custom_call" | custom-call | tf_op jit(solution)/shard_map/pallas_call | solution.py:282
  186.9 97.0 %shard_map.113 = f32[4,288,384]{2,1,0:T(8,128)S(1)} custom-call(bf16[4,288,512]{2,1,0:T(8,128)(2,1)S(1)} %shard_map.112.x_ref, bf16[4,8192,384]{2,1,0:T(8,128)(2,1)} %down_ref.1), custom_call_target="tpu_custom_call" | custom-call | tf_op jit(solution)/shard_map/pallas_call | solution.py:331
  284.0 0.4 add_convert_fusion
  284.4 0.0 copy-start.3
  284.4 1.0 copy.31
  285.4 3.6 %all-to-all-start.1 = ((bf16[4,2,144,384]{3,2,0,1:T(8,128)(2,1)}), bf16[4,2,144,384]{3,2,0,1:T(8,128)(2,1)S(1)}, u32[]{:S(2)}, u32[]{:S(2)}) async-start(bf16[4,2,144,384]{3,2,0,1:T(8,128)(2,1)} %copy.31), calls=%async_computation.1 | async-start | bytes 1769472 | tf_op jit(solution)/shard_map/all_to_all | solution.py:490
  288.9 0.0 copy-done.3
  289.0 11.0 %all-to-all-done.1 = bf16[4,2,144,384]{3,2,0,1:T(8,128)(2,1)S(1)} async-done(((bf16[4,2,144,384]{3,2,0,1:T(8,128)(2,1)}), bf16[4,2,144,384]{3,2,0,1:T(8,128)(2,1)S(1)}, u32[]{:S(2)}, u32[]{:S(2)}) %all-to-all-start.1) | async-done | bytes 884768 | tf_op jit(solution)/shard_map/all_to_all | solution.py:490
  300.0 1.6 fusion.13
  (10 shorter events, 0.1 us)
Async XLA Ops:
  0.0 29.0 %copy-start.5 = (s32[64]{0:T(128)S(1)}, s32[64]{0:T(128)}, u32[]{:S(2)}) copy-start(s32[64]{0:T(128)} %param.13) | copy-start | bytes 772
  0.0 29.2 %copy-start.1 = (bf16[64,3072]{1,0:T(8,128)(2,1)S(1)}, bf16[64,3072]{1,0:T(8,128)(2,1)}, u32[]{:S(2)}) copy-start(bf16[64,3072]{1,0:T(8,128)(2,1)} %q_ref.1) | copy-start | bytes 1179652
  29.0 8.2 %copy-start = (bf16[3072,384]{1,0:T(8,128)(2,1)S(1)}, bf16[3072,384]{1,0:T(8,128)(2,1)}, u32[]{:S(2)}) copy-start(bf16[3072,384]{1,0:T(8,128)(2,1)} %w_ref.1) | copy-start | bytes 7077892
  37.3 38.0 %copy-start.2 = (bf16[512,384]{1,0:T(8,128)(2,1)S(1)}, bf16[512,384]{1,0:T(8,128)(2,1)}, u32[]{:S(2)}) copy-start(bf16[512,384]{1,0:T(8,128)(2,1)} %param.14) | copy-start | bytes 1179652
  79.3 5.0 %copy-start.4 = (f32[1024,2]{0,1:T(2,128)S(1)}, f32[1024,2]{0,1:T(2,128)}, u32[]{:S(2)}) copy-start(f32[1024,2]{0,1:T(2,128)} %param.18) | copy-start | bytes 24580
  79.3 27.1 %all-to-all-start = ((bf16[8,288,384]{2,1,0:T(8,128)(2,1)}), bf16[8,288,384]{2,1,0:T(8,128)(2,1)}, u32[]{:S(2)}, u32[]{:S(2)}) async-start(bf16[8,288,384]{2,1,0:T(8,128)(2,1)} %bitcast.34), calls=%async_computation | async-start | bytes 3538944 | tf_op jit(solution)/shard_map/all_to_all | solution.py:445
  284.4 4.6 %copy-start.3 = (s32[1024,2]{0,1:T(2,128)S(1)}, s32[1024,2]{0,1:T(2,128)}, u32[]{:S(2)}) copy-start(s32[1024,2]{0,1:T(2,128)} %param.17) | copy-start | bytes 24580
  285.4 14.6 %all-to-all-start.1 = ((bf16[4,2,144,384]{3,2,0,1:T(8,128)(2,1)}), bf16[4,2,144,384]{3,2,0,1:T(8,128)(2,1)S(1)}, u32[]{:S(2)}, u32[]{:S(2)}) async-start(bf16[4,2,144,384]{3,2,0,1:T(8,128)(2,1)} %copy.31), calls=%async_computation.1 | async-start | bytes 1769472 | tf_op jit(solution)/shard_map/all_to_all | solution.py:490

commit v3 on v2

--- a/solution.py
+++ b/solution.py
@@ -262,7 +262,7 @@
                 au[e] += u
             return carry
 
-        lax.fori_loop(0, experts, one, 0)
+        lax.fori_loop(0, experts, one, 0, unroll=2)
 
     ring_gather(x_ref, buf, sems, consume, lambda me: fetch(me, 0))
 

time: 302 us -> 302 us (level)
  no operation moved by 1% of the time
where the time goes in v3:
time: 302 us; the launch traced here: 301 us
  Pallas kernels  243 us (80%)
  waiting for transfers between devices  30.8 us (10%)
  other arithmetic  9.77 us (3%)
  starting transfers between devices  8.55 us (3%)
  matrix products  5.4 us (2%)
  local copies, waits for them, and re-layouts  3.75 us (1%)
    pallas_call x1, Pallas kernels, ring_down(): pl.pallas_call(down_kernel, out_shape=jax.ShapeDtypeStruct((experts, coun...  97 us
    pallas_call x1, Pallas kernels, ring_hidden(): pl.pallas_call(functools.partial(hidden_kernel, gate_proj.shape[1]), out_...  78.2 us
    pallas_call x1, Pallas kernels, ring_project(): pl.pallas_call(project_kernel, out_shape=jax.ShapeDtypeStruct((RING_SIZE...  38 us
    pallas_call x1, Pallas kernels, gathered_rows(): pl.pallas_call(gather_kernel, out_shape=jax.ShapeDtypeStruct((RING_SIZE,)...  21.2 us
    all_to_all x1, waiting for transfers between devices, on_device(): lax.all_to_all(shares.astype(jnp.bfloat16).reshape(EXPERTS, width, feat_l...  19.9 us
    all_to_all x1, waiting for transfers between devices, on_device(): lax.all_to_all(payload.reshape(local_experts, n_blocks, capacity, feat_lo...  11 us
    pallas_call x1, Pallas kernels, local_attention(): pl.pallas_call(functools.partial(attention_kernel, scale), out_shape=jax....  8.1 us
  transfers between devices with their start and end apart: 2, of which 2 were waited for; matrix products, arithmetic and copies ran while one was open for 1% of the time, Pallas kernels for 0%

profile of v3, /device:TPU:0, one launch (start us, length us, event | category | flops | bytes accessed | tf_op | source)
XLA Modules:
  0.0 301.2 jit_solution(11163822515477214112)
XLA Ops:
  0.0 0.0 copy-start.5
  0.0 0.0 copy-start.1
  0.0 0.7 convert_bitcast_fusion
  0.7 0.1 copy.29
  0.8 0.8 reshape.88
  1.7 0.7 convert_reduce_fusion.1
  2.4 2.3 reduce-window.6
  4.7 0.3 slice_reduce_fusion
  5.0 0.1 bitcast_subtract_fusion
  5.1 0.7 select_reduce_fusion
  5.8 0.7 add_add_fusion
  6.5 0.9 copy.32
  7.5 0.1 fusion.23
  7.6 21.2 %shard_map.109 = bf16[16,64,1152]{2,1,0:T(8,128)(2,1)S(1)} custom-call(bf16[64,1152]{1,0:T(8,128)(2,1)S(1)} %pad_maximum_fusion.x_ref), custom_call_target="tpu_custom_call" | custom-call | tf_op jit(solution)/shard_map/pallas_call | solution.py:161
  28.8 0.2 convert_reduce_fusion
  29.0 0.0 copy-done.5
  29.0 0.0 copy-start
  29.1 0.1 fusion.20.bias_ref
  29.2 0.0 copy-done.1
  29.2 8.1 %shard_map.110.x_ref = bf16[64,3072]{1,0:T(8,128)(2,1)S(1)} custom-call(bf16[64,3072]{1,0:T(8,128)(2,1)S(1)} %copy-done.1, bf16[1024,1152]{1,0:T(8,128)(2,1)S(1)} %bitcast.31, f32[64,1024]{1,0:T(8,128)S(1)} %fusion.20.bias_ref), custom_call_target="tpu_custom_call" | custom-call | tf_op jit(solution)/shard_map/pallas_call | solution.py:219
  37.3 0.0 copy-done
  37.3 0.0 copy-start.2
  37.3 38.0 %shard_map.111 = f32[1024,384]{1,0:T(8,128)S(1)} custom-call(bf16[64,3072]{1,0:T(8,128)(2,1)S(1)} %shard_map.110.x_ref, bf16[3072,384]{1,0:T(8,128)(2,1)S(1)} %copy-done), custom_call_target="tpu_custom_call" | custom-call | tf_op jit(solution)/shard_map/pallas_call | solution.py:186
  75.3 0.0 copy-done.2
  75.3 0.1 add_dynamic-update-slice_fusion
  75.5 3.8 %fusion.7 = bf16[2304,384]{1,0:T(8,128)(2,1)} fusion(s32[1024]{0:T(1024)S(1)} %bitcast.43, s32[1024]{0:T(1024)S(1)} %bitcast.41, f32[1024,384]{1,0:T(8,128)S(1)} %add_dynamic-update-slice_fusion), kind=kOutput, calls=%fused_computation.10 | convolution fusion | flops 1820295168 | bytes 3350528 | tf_op jit(solution)/shard_map/dot_general | solution.py:444
  79.3 0.0 copy-start.4
  79.3 5.0 %all-to-all-start = ((bf16[8,288,384]{2,1,0:T(8,128)(2,1)}), bf16[8,288,384]{2,1,0:T(8,128)(2,1)}, u32[]{:S(2)}, u32[]{:S(2)}) async-start(bf16[8,288,384]{2,1,0:T(8,128)(2,1)} %bitcast.34), calls=%async_computation | async-start | bytes 3538944 | tf_op jit(solution)/shard_map/all_to_all | solution.py:445
  84.3 0.0 copy-done.4
  84.3 1.5 fusion.3
  85.8 0.1 mul.76
  85.9 0.1 mul.80
  86.0 0.1 slice_convert_fusion
  86.1 0.4 reshape.94.gain_ref
  86.5 19.9 %all-to-all-done = bf16[8,288,384]{2,1,0:T(8,128)(2,1)} async-done(((bf16[8,288,384]{2,1,0:T(8,128)(2,1)}), bf16[8,288,384]{2,1,0:T(8,128)(2,1)}, u32[]{:S(2)}, u32[]{:S(2)}) %all-to-all-start) | async-done | bytes 1769504 | tf_op jit(solution)/shard_map/all_to_all | solution.py:445
  106.4 1.9 reduce_sum.51.x_ref
  108.3 78.2 %shard_map.112.x_ref = bf16[4,288,512]{2,1,0:T(8,128)(2,1)S(1)} custom-call(bf16[4,288,384]{2,1,0:T(8,128)(2,1)S(1)} %reduce_sum.51.x_ref, f32[16,1,384]{2,1,0:T(1,128)S(1)} %reshape.94.gain_ref, bf16[4,6144,512]{2,1,0:T(8,128)(2,1)} %gate_ref.1, bf16[4,6144,512]{2,1,0:T(8,128)(2,1)} %up_ref.1), custom_call_target="tpu_custom_call" | custom-call | tf_op jit(solution)/shard_map/pallas_call | solution.py:282
  186.5 97.0 %shard_map.113 = f32[4,288,384]{2,1,0:T(8,128)S(1)} custom-call(bf16[4,288,512]{2,1,0:T(8,128)(2,1)S(1)} %shard_map.112.x_ref, bf16[4,8192,384]{2,1,0:T(8,128)(2,1)} %down_ref.1), custom_call_target="tpu_custom_call" | custom-call | tf_op jit(solution)/shard_map/pallas_call | solution.py:331
  283.6 0.4 add_convert_fusion
  284.0 0.0 copy-start.3
  284.0 1.0 copy.31
  285.0 3.6 %all-to-all-start.1 = ((bf16[4,2,144,384]{3,2,0,1:T(8,128)(2,1)}), bf16[4,2,144,384]{3,2,0,1:T(8,128)(2,1)S(1)}, u32[]{:S(2)}, u32[]{:S(2)}) async-start(bf16[4,2,144,384]{3,2,0,1:T(8,128)(2,1)} %copy.31), calls=%async_computation.1 | async-start | bytes 1769472 | tf_op jit(solution)/shard_map/all_to_all | solution.py:490
  288.5 0.0 copy-done.3
  288.6 11.0 %all-to-all-done.1 = bf16[4,2,144,384]{3,2,0,1:T(8,128)(2,1)S(1)} async-done(((bf16[4,2,144,384]{3,2,0,1:T(8,128)(2,1)}), bf16[4,2,144,384]{3,2,0,1:T(8,128)(2,1)S(1)}, u32[]{:S(2)}, u32[]{:S(2)}) %all-to-all-start.1) | async-done | bytes 884768 | tf_op jit(solution)/shard_map/all_to_all | solution.py:490
  299.5 1.6 fusion.13
  (10 shorter events, 0.1 us)
Async XLA Ops:
  0.0 29.0 %copy-start.5 = (s32[64]{0:T(128)S(1)}, s32[64]{0:T(128)}, u32[]{:S(2)}) copy-start(s32[64]{0:T(128)} %param.13) | copy-start | bytes 772
  0.0 29.2 %copy-start.1 = (bf16[64,3072]{1,0:T(8,128)(2,1)S(1)}, bf16[64,3072]{1,0:T(8,128)(2,1)}, u32[]{:S(2)}) copy-start(bf16[64,3072]{1,0:T(8,128)(2,1)} %q_ref.1) | copy-start | bytes 1179652
  29.0 8.2 %copy-start = (bf16[3072,384]{1,0:T(8,128)(2,1)S(1)}, bf16[3072,384]{1,0:T(8,128)(2,1)}, u32[]{:S(2)}) copy-start(bf16[3072,384]{1,0:T(8,128)(2,1)} %w_ref.1) | copy-start | bytes 7077892
  37.3 38.0 %copy-start.2 = (bf16[512,384]{1,0:T(8,128)(2,1)S(1)}, bf16[512,384]{1,0:T(8,128)(2,1)}, u32[]{:S(2)}) copy-start(bf16[512,384]{1,0:T(8,128)(2,1)} %param.14) | copy-start | bytes 1179652
  79.3 5.0 %copy-start.4 = (f32[1024,2]{0,1:T(2,128)S(1)}, f32[1024,2]{0,1:T(2,128)}, u32[]{:S(2)}) copy-start(f32[1024,2]{0,1:T(2,128)} %param.18) | copy-start | bytes 24580
  79.3 27.1 %all-to-all-start = ((bf16[8,288,384]{2,1,0:T(8,128)(2,1)}), bf16[8,288,384]{2,1,0:T(8,128)(2,1)}, u32[]{:S(2)}, u32[]{:S(2)}) async-start(bf16[8,288,384]{2,1,0:T(8,128)(2,1)} %bitcast.34), calls=%async_computation | async-start | bytes 3538944 | tf_op jit(solution)/shard_map/all_to_all | solution.py:445
  284.0 4.6 %copy-start.3 = (s32[1024,2]{0,1:T(2,128)S(1)}, s32[1024,2]{0,1:T(2,128)}, u32[]{:S(2)}) copy-start(s32[1024,2]{0,1:T(2,128)} %param.17) | copy-start | bytes 24580
  285.0 14.6 %all-to-all-start.1 = ((bf16[4,2,144,384]{3,2,0,1:T(8,128)(2,1)}), bf16[4,2,144,384]{3,2,0,1:T(8,128)(2,1)S(1)}, u32[]{:S(2)}, u32[]{:S(2)}) async-start(bf16[4,2,144,384]{3,2,0,1:T(8,128)(2,1)} %copy.31), calls=%async_computation.1 | async-start | bytes 1769472 | tf_op jit(solution)/shard_map/all_to_all | solution.py:490
